TPU v7x, 256 devices: a whole 4x4x8 slice. The times are simulated.
256 devices in a mesh: az: 16 (over y_lo, z), tm: 16 (over y_hi, x, core).
Axes of the slice: x: 4, y: 4 (y_hi: 2, y_lo: 2; y = y_hi * 2 + y_lo), z: 8, core: 2. Of those that a mesh axis runs over, the one named last changes fastest.
Arguments:
- teacher_q: bfloat16 [16, 2048, 2560], P('az', 'tm'), may hold values from -6 to 6
- teacher_k: bfloat16 [16, 2048, 2560], P('az', 'tm'), may hold values from -6 to 6
- teacher_v: bfloat16 [16, 2048, 2560], P('az', 'tm'), may hold values from -96 to 96
- band: int32 [16, 16], P('tm', 'az'), may hold values from 0 to 4, as said below
- head_mix: float32 [20, 8], replicated, may hold values from -1.25 to 1.25
- latents: bfloat16 [16, 2048, 1024], P('az', 'tm'), may hold values from -6 to 6
- w_qk: bfloat16 [1024, 2048], replicated, may hold values from -0.1875 to 0.1875
- w_v: bfloat16 [1024, 1024], replicated, may hold values from -1.5 to 1.5
Outputs:
- gap: float32 [16, 2048, 1024], P('az', 'tm')
Inputs may be any that keep to these rules, and one draw needn't show every extreme that they name: `band`: every time block has at least one azimuth block whose half-width is 4.
All inputs are finite; a program needn't handle non-finite values.
Results may differ from a plain program's by a relative error of at most 0.0052.
Values may be sent and summed in bfloat16 or wider, within the bound.
A program may use at most 128 MiB of HBM per device.

v0:
```python
import math

import jax
import jax.numpy as jnp
from jax import lax
from jax.sharding import PartitionSpec as P


def shifted(array, axis, by):
    size = lax.axis_size(axis)
    return lax.ppermute(array, axis, [(i, (i + by) % size) for i in range(size)])


def with_halo(block, sides, width):
    for axis, dim in sides:
        count = lax.axis_size(axis)
        forward = [(i, i + 1) for i in range(count - 1)]
        backward = [(target, source) for source, target in forward]
        low = lax.ppermute(
            lax.slice_in_dim(block, block.shape[dim] - width, None, axis=dim), axis, forward
        )
        high = lax.ppermute(lax.slice_in_dim(block, 0, width, axis=dim), axis, backward)
        block = jnp.concatenate([low, block, high], axis=dim)
    return block


def headnorm(u, heads):
    shaped = u.reshape(u.shape[0], heads, u.shape[-1] // heads)
    return shaped * lax.rsqrt(jnp.mean(shaped * shaped, axis=-1, keepdims=True) + 1e-06)


def shards(teacher_q, teacher_k, teacher_v, band, head_mix, latents, w_qk, w_v):
    tokens = teacher_q.shape[1]
    width = teacher_q.shape[2]
    heads_t = head_mix.shape[0]
    heads_s = head_mix.shape[1]
    head_dim = width // heads_t
    scale = 1.0 / math.sqrt(head_dim)
    queries = headnorm(teacher_q[0].astype(jnp.float32), heads_t).astype(jnp.bfloat16)
    keys_own = (
        headnorm(teacher_k[0].astype(jnp.float32), heads_t)
        .astype(jnp.bfloat16)
        .reshape(tokens, width)
    )
    values_own = teacher_v[0]
    reach = band[0, 0]
    az_count = lax.axis_size("az")

    def attend(carry, keys, values, keep):
        total, accum = carry
        rows = keys.shape[0]
        scores = (
            jnp.einsum(
                "qhd,khd->hqk",
                queries,
                keys.reshape(rows, heads_t, head_dim),
                preferred_element_type=jnp.float32,
            )
            * scale
        )
        probs = jnp.exp(scores) * keep[None, None, :]
        total = total + jnp.sum(probs, axis=-1)
        accum = accum + jnp.einsum(
            "hqk,khd->hqd",
            probs.astype(jnp.bfloat16),
            values.reshape(rows, heads_t, head_dim),
            preferred_element_type=jnp.float32,
        )
        return (total, accum)

    def tile(carry, keys, values, keep):
        return attend(carry, keys, values, keep)

    initial = (
        jnp.zeros((heads_t, tokens), jnp.float32),
        jnp.zeros((heads_t, tokens, head_dim), jnp.float32),
    )
    ones = jnp.ones((tokens,), jnp.float32)
    carry = tile(initial, keys_own, values_own, ones)
    ahead = jnp.stack([keys_own, values_own])
    behind = ahead
    for step in range(1, az_count // 4 + 1):
        ahead = shifted(ahead, "az", 1)
        behind = shifted(behind, "az", -1)
        keep = jnp.where(step <= reach, 1.0, 0.0) * ones
        carry = tile(carry, ahead[0], ahead[1], keep)
        carry = tile(carry, behind[0], behind[1], keep)
    total, accum = carry
    tout = accum / total[..., None]
    target = jnp.einsum("hqd,hs->qsd", tout, head_mix, precision=lax.Precision.HIGHEST).reshape(
        tokens, heads_s * head_dim
    )
    rows_in = latents[0]
    student_width = w_v.shape[0]
    qk = jnp.dot(rows_in, w_qk, preferred_element_type=jnp.float32)
    sv = jnp.dot(rows_in, w_v, preferred_element_type=jnp.float32)
    snq = headnorm(qk[:, :student_width], heads_s).astype(jnp.bfloat16)
    snk = (
        headnorm(qk[:, student_width:], heads_s).astype(jnp.bfloat16).reshape(tokens, student_width)
    )
    svr = sv.astype(jnp.bfloat16)
    window = tokens // 2
    extended = with_halo(jnp.stack([snk, svr]), (("tm", 1),), window)
    span = tokens + 2 * window
    base = lax.axis_index("tm") * tokens
    limit = lax.axis_size("tm") * tokens
    pos_q = base + jnp.arange(tokens, dtype=jnp.int32)[:, None]
    pos_k = base - window + jnp.arange(span, dtype=jnp.int32)[None, :]
    keep = (jnp.abs(pos_q - pos_k) <= window) & (pos_k >= 0) & (pos_k < limit)
    scores = (
        jnp.einsum(
            "qhd,khd->hqk",
            snq,
            extended[0].reshape(span, heads_s, head_dim),
            preferred_element_type=jnp.float32,
        )
        * scale
    )
    probs = jnp.where(keep[None], jnp.exp(scores), 0.0)
    stotal = jnp.sum(probs, axis=-1)
    saccum = jnp.einsum(
        "hqk,khd->hqd",
        probs.astype(jnp.bfloat16),
        extended[1].reshape(span, heads_s, head_dim),
        preferred_element_type=jnp.float32,
    )
    sout = jnp.transpose(saccum / stotal[..., None], (1, 0, 2)).reshape(tokens, student_width)
    return (sout - target)[None]


def solution(mesh):
    in_specs = (
        P("az", "tm", None),
        P("az", "tm", None),
        P("az", "tm", None),
        P("tm", "az"),
        P(),
        P("az", "tm", None),
        P(),
        P(),
    )
    out_specs = P("az", "tm", None)
    return jax.shard_map(shards, mesh=mesh, in_specs=in_specs, out_specs=out_specs, check_vma=False)
```

profile of v0, /device:TPU:14, one launch (start us, length us, event | category | flops | bytes accessed | tf_op | source)
XLA Modules:
  0.0 158.6 jit_solution(3891660431012185658)
XLA Ops:
  0.0 2.3 %copy.100 = bf16[1,128,2560]{1,2,0:T(8,128)(2,1)} copy(bf16[1,128,2560]{2,1,0:T(8,128)(2,1)} %param.9) | data formatting | bytes 1310720 | tf_op args[1]
  2.3 0.3 copy.103
  2.7 1.6 %copy.99 = bf16[1,128,2560]{1,2,0:T(8,128)(2,1)S(1)} copy(bf16[1,128,2560]{2,1,0:T(8,128)(2,1)} %param.8) | data formatting | bytes 1310720 | tf_op args[0]
  4.3 0.1 fusion.25
  4.5 2.6 %multiply_reduce_fusion = (f32[128,20]{0,1:T(8,128)S(1)}, f32[128,20,128]{0,2,1:T(8,128)}) fusion(bf16[128,20,128]{0,2,1:T(8,128)(2,1)} %bitcast.111), kind=kLoop, calls=%fused_computation.48 | loop fusion | flops 980480 | bytes 1976320 | tf_op jit(solution)/shard_map/reduce_sum | solution.py:29
  7.1 0.6 add_rsqrt_fusion
  7.9 1.2 pad_maximum_fusion
  9.0 5.7 %collective-permute-start.3 = (bf16[2,128,2560]{1,2,0:T(8,128)(2,1)}, bf16[2,128,2560]{1,2,0:T(8,128)(2,1)}, u32[]{:S(2)}, u32[]{:S(2)}) collective-permute-start(bf16[2,128,2560]{1,2,0:T(8,128)(2,1)} %pad_maximum_fusion), channel_id=1, source_target_pairs={{0,240},{16,0},{32,16},{48,32},{64,48},{80,64},{96,80},{112,96},{1... | collective-permute-start | bytes 3932168 | tf_op jit(solution)/shard_map/ppermute | solution.py:11
  14.8 0.5 fusion.30
  15.3 0.7 fusion.51
  16.0 0.9 copy.180
  16.9 1.2 reduce_sum.127
  18.4 0.2 mul.166
  18.6 1.0 slice_bitcast_fusion.1
  19.6 1.9 %fusion.48 = (bf16[2,64,1024]{2,1,0:T(8,128)(2,1)}, bf16[2,64,1024]{2,1,0:T(8,128)(2,1)}) fusion(bf16[1,128,1024]{2,1,0:T(8,128)(2,1)} %get-tuple-element.24, bf16[1,128,1024]{2,1,0:T(8,128)(2,1)S(1)} %fusion.30), kind=kLoop, calls=%fused_computation.80 | loop fusion | flops 1048576 | bytes 1048576 | tf_op jit(solution)/shard_map/stack | solution.py:103
  21.5 1.9 %collective-permute-start = (bf16[2,64,1024]{2,1,0:T(8,128)(2,1)}, bf16[2,64,1024]{2,1,0:T(8,128)(2,1)}, u32[]{:S(2)}, u32[]{:S(2)}) collective-permute-start(bf16[2,64,1024]{2,1,0:T(8,128)(2,1)} %get-tuple-element.27), channel_id=1, source_target_pairs={{0,1},{1,2},{2,3},{3,4},{4,5},{5,6},{6,7},{7,8},{8,9},{9,10},{10,1... | collective-permute-start | bytes 786440 | tf_op jit(solution)/shard_map/ppermute | solution.py:19
  23.4 3.6 %collective-permute-start.1 = (bf16[2,64,1024]{2,1,0:T(8,128)(2,1)}, bf16[2,64,1024]{2,1,0:T(8,128)(2,1)}, u32[]{:S(2)}, u32[]{:S(2)}) collective-permute-start(bf16[2,64,1024]{2,1,0:T(8,128)(2,1)} %get-tuple-element.28), channel_id=1, source_target_pairs={{1,0},{2,1},{3,2},{4,3},{5,4},{6,5},{7,6},{8,7},{9,8},{10,9},{11,1... | collective-permute-start | bytes 786440 | tf_op jit(solution)/shard_map/ppermute | solution.py:22
  27.0 0.5 iota_add_fusion.1
  27.5 0.6 iota_add_fusion
  28.1 0.6 fusion.57
  28.7 1.1 copy.179
  29.9 0.8 multiply_reduce_fusion.1
  30.7 0.9 copy.92
  31.6 2.5 %fusion.83 = (f32[20,128]{1,0:T(8,128)}, bf16[20,128,128]{1,2,0:T(8,128)(2,1)S(1)}) fusion(f32[128,20,128]{0,2,1:T(8,128)} %get-tuple-element.6, f32[128,20]{0,1:T(8,128)S(1)} %get-tuple-element.49, bf16[128,20,128]{0,2,1:T(8,128)(2,1)S(1)} %bitcast.102, f32[128,20]{0,1:T(8,128)} %get-tuple-element.50), kind=kOutput, calls=%fused_computation.115 | convolution fusion | flops 86504960 | bytes 2652160 | tf_op jit(solution)/shard_map/qhd,khd->hqk/dot_general | solution.py:53
  34.1 1.7 %fusion.42 = f32[20,128,128]{2,1,0:T(8,128)} fusion(bf16[128,20,128]{0,2,1:T(8,128)(2,1)S(1)} %bitcast.100, bf16[20,128,128]{1,2,0:T(8,128)(2,1)S(1)} %get-tuple-element.44), kind=kOutput, calls=%fused_computation.66 | convolution fusion | flops 83886080 | bytes 2621440 | tf_op jit(solution)/shard_map/hqk,khd->hqd/dot_general | solution.py:63
  35.8 0.7 fusion.55
  37.3 0.7 copy.93
  38.0 1.8 %multiply_convert_fusion.2 = bf16[128,8,128]{2,1,0:T(8,128)(2,1)} fusion(f32[128,8]{1,0:T(8,128)} %copy.93, f32[16,8,8,128]{3,2,1,0:T(8,128)S(1)} %copy.179), kind=kLoop, calls=%fused_computation.78 | loop fusion | flops 262144 | bytes 790528 | tf_op jit(solution)/shard_map/convert_element_type | solution.py:97
  39.7 1.2 pad_maximum_fusion.1
  41.0 0.9 copy.182
  41.9 1.0 copy.178
  42.9 2.2 %fusion.85 = (f32[8,128]{1,0:T(8,128)S(1)}, bf16[8,128,256]{2,1,0:T(8,128)(2,1)}) fusion(bf16[256,8,128]{2,1,0:T(8,128)(2,1)} %bitcast.132, bf16[128,8,128]{2,1,0:T(8,128)(2,1)S(1)} %copy-done.11, pred[128,256]{1,0:T(8,128)(4,1)} %fusion.55), kind=kOutput, calls=%fused_computation.117 | convolution fusion | flops 68156416 | bytes 1347584 | tf_op jit(solution)/shard_map/qhd,khd->hqk/dot_general | solution.py:111
  45.2 4.1 %collective-permute-start.5 = (bf16[2,128,2560]{1,2,0:T(8,128)(2,1)}, bf16[2,128,2560]{1,2,0:T(8,128)(2,1)S(1)}, u32[]{:S(2)}, u32[]{:S(2)}) collective-permute-start(bf16[2,128,2560]{1,2,0:T(8,128)(2,1)} %collective-permute-done.3), channel_id=1, source_target_pairs={{0,240},{16,0},{32,16},{48,32},{64,48},{80,64},{96,80},{112,96},{1... | collective-permute-start | bytes 3932168 | tf_op jit(solution)/shard_map/ppermute | solution.py:11
  49.3 1.4 fusion.71
  50.7 1.4 fusion.72
  52.2 0.6 fusion.82
  52.7 0.5 fusion.84
  53.3 0.8 copy-done.6
  54.0 0.6 convolution_add_fusion.4
  54.6 0.6 convolution_add_fusion.3
  55.3 23.1 %collective-permute-done.5 = bf16[2,128,2560]{1,2,0:T(8,128)(2,1)S(1)} collective-permute-done((bf16[2,128,2560]{1,2,0:T(8,128)(2,1)}, bf16[2,128,2560]{1,2,0:T(8,128)(2,1)S(1)}, u32[]{:S(2)}, u32[]{:S(2)}) %collective-permute-start.5) | collective-permute-done | bytes 1310752 | tf_op jit(solution)/shard_map/ppermute | solution.py:11
  78.3 4.5 %collective-permute-start.7 = (bf16[2,128,2560]{1,2,0:T(8,128)(2,1)S(1)}, bf16[2,128,2560]{1,2,0:T(8,128)(2,1)S(1)}, u32[]{:S(2)}, u32[]{:S(2)}) collective-permute-start(bf16[2,128,2560]{1,2,0:T(8,128)(2,1)S(1)} %collective-permute-done.5), channel_id=1, source_target_pairs={{0,240},{16,0},{32,16},{48,32},{64,48},{80,64},{96,80},{112,96},{1... | collective-permute-start | bytes 3932168 | tf_op jit(solution)/shard_map/ppermute | solution.py:11
  82.9 0.5 fusion.80
  83.4 0.6 fusion.37
  84.1 1.8 %collective-permute-done.4 = bf16[2,128,2560]{1,2,0:T(8,128)(2,1)S(1)} collective-permute-done((bf16[2,128,2560]{1,2,0:T(8,128)(2,1)}, bf16[2,128,2560]{1,2,0:T(8,128)(2,1)S(1)}, u32[]{:S(2)}, u32[]{:S(2)}) %collective-permute-start.4) | collective-permute-done | bytes 1310752 | tf_op jit(solution)/shard_map/ppermute | solution.py:11
  86.0 0.5 fusion.81
  86.5 0.6 fusion.15
  87.1 24.2 %collective-permute-done.7 = bf16[2,128,2560]{1,2,0:T(8,128)(2,1)S(1)} collective-permute-done((bf16[2,128,2560]{1,2,0:T(8,128)(2,1)S(1)}, bf16[2,128,2560]{1,2,0:T(8,128)(2,1)S(1)}, u32[]{:S(2)}, u32[]{:S(2)}) %collective-permute-start.7) | collective-permute-done | bytes 1310752 | tf_op jit(solution)/shard_map/ppermute | solution.py:11
  111.3 4.6 %collective-permute-start.9 = (bf16[2,128,2560]{1,2,0:T(8,128)(2,1)S(1)}, bf16[2,128,2560]{1,2,0:T(8,128)(2,1)S(1)}, u32[]{:S(2)}, u32[]{:S(2)}) collective-permute-start(bf16[2,128,2560]{1,2,0:T(8,128)(2,1)S(1)} %collective-permute-done.7), channel_id=1, source_target_pairs={{0,240},{16,0},{32,16},{48,32},{64,48},{80,64},{96,80},{112,96},{1... | collective-permute-start | bytes 3932168 | tf_op jit(solution)/shard_map/ppermute | solution.py:11
  116.0 2.8 %collective-permute-done.6 = bf16[2,128,2560]{1,2,0:T(8,128)(2,1)S(1)} collective-permute-done((bf16[2,128,2560]{1,2,0:T(8,128)(2,1)S(1)}, bf16[2,128,2560]{1,2,0:T(8,128)(2,1)S(1)}, u32[]{:S(2)}, u32[]{:S(2)}) %collective-permute-start.6) | collective-permute-done | bytes 1310752 | tf_op jit(solution)/shard_map/ppermute | solution.py:11
  118.9 0.5 fusion.78
  119.5 0.6 fusion.79
  120.1 0.6 fusion.34
  120.7 0.6 fusion.10
  121.3 22.3 %collective-permute-done.9 = bf16[2,128,2560]{1,2,0:T(8,128)(2,1)S(1)} collective-permute-done((bf16[2,128,2560]{1,2,0:T(8,128)(2,1)S(1)}, bf16[2,128,2560]{1,2,0:T(8,128)(2,1)S(1)}, u32[]{:S(2)}, u32[]{:S(2)}) %collective-permute-start.9) | collective-permute-done | bytes 1310752 | tf_op jit(solution)/shard_map/ppermute | solution.py:11
  143.6 0.5 fusion.76
  144.2 6.8 %collective-permute-done.8 = bf16[2,128,2560]{1,2,0:T(8,128)(2,1)S(1)} collective-permute-done((bf16[2,128,2560]{1,2,0:T(8,128)(2,1)S(1)}, bf16[2,128,2560]{1,2,0:T(8,128)(2,1)S(1)}, u32[]{:S(2)}, u32[]{:S(2)}) %collective-permute-start.8) | collective-permute-done | bytes 1310752 | tf_op jit(solution)/shard_map/ppermute | solution.py:11
  151.1 0.5 fusion.77
  151.7 0.6 fusion.31
  152.4 0.8 fusion.5
  153.2 1.8 %fusion = f32[128,128,8]{1,2,0:T(8,128)S(1)} fusion(f32[20,128,128]{2,1,0:T(8,128)S(1)} %fusion.5, f32[20,8]{0,1:T(8,128)S(1)} %copy-done.14), kind=kOutput, calls=%fused_computation.2 | convolution fusion | flops 31457280 | bytes 1835648 | tf_op jit(solution)/shard_map/hqd,hs->qsd/dot_general | solution.py:90
  155.1 1.0 copy.140
  156.1 1.5 fusion.29
  157.6 1.0 copy.141
  (59 shorter events, 1.3 us)
Async XLA Ops:
  0.0 14.8 %copy-start = (bf16[1024,1024]{1,0:T(8,128)(2,1)S(1)}, bf16[1024,1024]{1,0:T(8,128)(2,1)}, u32[]{:S(2)}) copy-start(bf16[1024,1024]{1,0:T(8,128)(2,1)} %param.15) | copy-start | bytes 6291460
  0.0 2.3 %copy-start.9 = (bf16[1,128,2560]{2,1,0:T(8,128)(2,1)S(1)}, bf16[1,128,2560]{2,1,0:T(8,128)(2,1)}, u32[]{:S(2)}) copy-start(bf16[1,128,2560]{2,1,0:T(8,128)(2,1)} %param.10) | copy-start | bytes 1966084
  2.7 5.2 %copy-start.1 = (bf16[1,128,2560]{1,2,0:T(8,128)(2,1)}, bf16[1,128,2560]{1,2,0:T(8,128)(2,1)S(1)}, u32[]{:S(2)}) copy-start(bf16[1,128,2560]{1,2,0:T(8,128)(2,1)S(1)} %copy.103) | copy-start | bytes 1966084
  4.3 2.8 %copy-start.3 = (bf16[1,128,2560]{1,2,0:T(8,128)(2,1)}, bf16[1,128,2560]{1,2,0:T(8,128)(2,1)S(1)}, u32[]{:S(2)}) copy-start(bf16[1,128,2560]{1,2,0:T(8,128)(2,1)S(1)} %copy.99) | copy-start | bytes 1966084
  4.3 3.4 %copy-start.5 = (bf16[1,128,2560]{1,2,0:T(8,128)(2,1)S(1)}, bf16[1,128,2560]{1,2,0:T(8,128)(2,1)}, u32[]{:S(2)}) copy-start(bf16[1,128,2560]{1,2,0:T(8,128)(2,1)} %copy.100) | copy-start | bytes 1966084
  7.7 7.1 %copy-start.8 = (bf16[1,128,1024]{2,1,0:T(8,128)(2,1)S(1)}, bf16[1,128,1024]{2,1,0:T(8,128)(2,1)}, u32[]{:S(2)}) copy-start(bf16[1,128,1024]{2,1,0:T(8,128)(2,1)} %param.13) | copy-start | bytes 786436
  7.8 7.4 %copy-start.7 = (bf16[1024,2048]{1,0:T(8,128)(2,1)S(1)}, bf16[1024,2048]{1,0:T(8,128)(2,1)}, u32[]{:S(2)}) copy-start(bf16[1024,2048]{1,0:T(8,128)(2,1)} %param.14) | copy-start | bytes 12582916
  9.0 36.1 %collective-permute-start.3 = (bf16[2,128,2560]{1,2,0:T(8,128)(2,1)}, bf16[2,128,2560]{1,2,0:T(8,128)(2,1)}, u32[]{:S(2)}, u32[]{:S(2)}) collective-permute-start(bf16[2,128,2560]{1,2,0:T(8,128)(2,1)} %pad_maximum_fusion), channel_id=1, source_target_pairs={{0,240},{16,0},{32,16},{48,32},{64,48},{80,64},{96,80},{112,96},{1... | collective-permute-start | bytes 3932168 | tf_op jit(solution)/shard_map/ppermute | solution.py:11
  14.8 35.9 %collective-permute-start.2 = (bf16[2,128,2560]{1,2,0:T(8,128)(2,1)}, bf16[2,128,2560]{1,2,0:T(8,128)(2,1)}, u32[]{:S(2)}, u32[]{:S(2)}) collective-permute-start(bf16[2,128,2560]{1,2,0:T(8,128)(2,1)} %pad_maximum_fusion), channel_id=1, source_target_pairs={{0,16},{16,32},{32,48},{48,64},{64,80},{80,96},{96,112},{112,128},... | collective-permute-start | bytes 3932168 | tf_op jit(solution)/shard_map/ppermute | solution.py:11
  19.6 12.0 %copy-start.4 = (bf16[1,128,2560]{1,2,0:T(8,128)(2,1)S(1)}, bf16[1,128,2560]{1,2,0:T(8,128)(2,1)}, u32[]{:S(2)}) copy-start(bf16[1,128,2560]{1,2,0:T(8,128)(2,1)} %copy-done.3) | copy-start | bytes 1966084
  21.5 18.3 %collective-permute-start = (bf16[2,64,1024]{2,1,0:T(8,128)(2,1)}, bf16[2,64,1024]{2,1,0:T(8,128)(2,1)}, u32[]{:S(2)}, u32[]{:S(2)}) collective-permute-start(bf16[2,64,1024]{2,1,0:T(8,128)(2,1)} %get-tuple-element.27), channel_id=1, source_target_pairs={{0,1},{1,2},{2,3},{3,4},{4,5},{5,6},{6,7},{7,8},{8,9},{9,10},{10,1... | collective-permute-start | bytes 786440 | tf_op jit(solution)/shard_map/ppermute | solution.py:19
  23.4 16.4 %collective-permute-start.1 = (bf16[2,64,1024]{2,1,0:T(8,128)(2,1)}, bf16[2,64,1024]{2,1,0:T(8,128)(2,1)}, u32[]{:S(2)}, u32[]{:S(2)}) collective-permute-start(bf16[2,64,1024]{2,1,0:T(8,128)(2,1)} %get-tuple-element.28), channel_id=1, source_target_pairs={{1,0},{2,1},{3,2},{4,3},{5,4},{6,5},{7,6},{8,7},{9,8},{10,9},{11,1... | collective-permute-start | bytes 786440 | tf_op jit(solution)/shard_map/ppermute | solution.py:22
  31.6 2.5 %copy-start.2 = (bf16[1,128,2560]{1,2,0:T(8,128)(2,1)S(1)}, bf16[1,128,2560]{1,2,0:T(8,128)(2,1)}, u32[]{:S(2)}) copy-start(bf16[1,128,2560]{1,2,0:T(8,128)(2,1)} %copy-done.1) | copy-start | bytes 1966084
  34.1 1.7 %copy-start.15 = (s32[256]{0:T(256)S(1)}, s32[256]{0:T(256)}, u32[]{:S(2)}) copy-start(s32[256]{0:T(256)} %iota_add_fusion) | copy-start | bytes 3076
  34.1 1.7 %copy-start.16 = (s32[128]{0:T(128)S(1)}, s32[128]{0:T(128)}, u32[]{:S(2)}) copy-start(s32[128]{0:T(128)} %iota_add_fusion.1) | copy-start | bytes 1540
  34.1 1.7 %copy-start.17 = (pred[256]{0:T(512)(128)(4,1)S(1)}, pred[256]{0:T(512)(128)(4,1)}, u32[]{:S(2)}) copy-start(pred[256]{0:T(512)(128)(4,1)} %get-tuple-element.51) | copy-start | bytes 772
  34.1 1.7 %copy-start.18 = (pred[256]{0:T(512)(128)(4,1)S(1)}, pred[256]{0:T(512)(128)(4,1)}, u32[]{:S(2)}) copy-start(pred[256]{0:T(512)(128)(4,1)} %get-tuple-element.52) | copy-start | bytes 772
  41.0 1.9 %copy-start.11 = (bf16[128,8,128]{2,1,0:T(8,128)(2,1)S(1)}, bf16[128,8,128]{2,1,0:T(8,128)(2,1)}, u32[]{:S(2)}) copy-start(bf16[128,8,128]{2,1,0:T(8,128)(2,1)} %multiply_convert_fusion.2) | copy-start | bytes 786436
  45.2 33.1 %collective-permute-start.5 = (bf16[2,128,2560]{1,2,0:T(8,128)(2,1)}, bf16[2,128,2560]{1,2,0:T(8,128)(2,1)S(1)}, u32[]{:S(2)}, u32[]{:S(2)}) collective-permute-start(bf16[2,128,2560]{1,2,0:T(8,128)(2,1)} %collective-permute-done.3), channel_id=1, source_target_pairs={{0,240},{16,0},{32,16},{48,32},{64,48},{80,64},{96,80},{112,96},{1... | collective-permute-start | bytes 3932168 | tf_op jit(solution)/shard_map/ppermute | solution.py:11
  50.7 1.5 copy-start.12
  52.1 33.8 %collective-permute-start.4 = (bf16[2,128,2560]{1,2,0:T(8,128)(2,1)}, bf16[2,128,2560]{1,2,0:T(8,128)(2,1)S(1)}, u32[]{:S(2)}, u32[]{:S(2)}) collective-permute-start(bf16[2,128,2560]{1,2,0:T(8,128)(2,1)} %collective-permute-done.2), channel_id=1, source_target_pairs={{0,16},{16,32},{32,48},{48,64},{64,80},{80,96},{96,112},{112,128},... | collective-permute-start | bytes 3932168 | tf_op jit(solution)/shard_map/ppermute | solution.py:11
  52.7 1.3 copy-start.6
  78.3 33.0 %collective-permute-start.7 = (bf16[2,128,2560]{1,2,0:T(8,128)(2,1)S(1)}, bf16[2,128,2560]{1,2,0:T(8,128)(2,1)S(1)}, u32[]{:S(2)}, u32[]{:S(2)}) collective-permute-start(bf16[2,128,2560]{1,2,0:T(8,128)(2,1)S(1)} %collective-permute-done.5), channel_id=1, source_target_pairs={{0,240},{16,0},{32,16},{48,32},{64,48},{80,64},{96,80},{112,96},{1... | collective-permute-start | bytes 3932168 | tf_op jit(solution)/shard_map/ppermute | solution.py:11
  85.9 32.9 %collective-permute-start.6 = (bf16[2,128,2560]{1,2,0:T(8,128)(2,1)S(1)}, bf16[2,128,2560]{1,2,0:T(8,128)(2,1)S(1)}, u32[]{:S(2)}, u32[]{:S(2)}) collective-permute-start(bf16[2,128,2560]{1,2,0:T(8,128)(2,1)S(1)} %collective-permute-done.4), channel_id=1, source_target_pairs={{0,16},{16,32},{32,48},{48,64},{64,80},{80,96},{96,112},{112,128},... | collective-permute-start | bytes 3932168 | tf_op jit(solution)/shard_map/ppermute | solution.py:11
  111.3 32.3 %collective-permute-start.9 = (bf16[2,128,2560]{1,2,0:T(8,128)(2,1)S(1)}, bf16[2,128,2560]{1,2,0:T(8,128)(2,1)S(1)}, u32[]{:S(2)}, u32[]{:S(2)}) collective-permute-start(bf16[2,128,2560]{1,2,0:T(8,128)(2,1)S(1)} %collective-permute-done.7), channel_id=1, source_target_pairs={{0,240},{16,0},{32,16},{48,32},{64,48},{80,64},{96,80},{112,96},{1... | collective-permute-start | bytes 3932168 | tf_op jit(solution)/shard_map/ppermute | solution.py:11
  118.9 32.2 %collective-permute-start.8 = (bf16[2,128,2560]{1,2,0:T(8,128)(2,1)S(1)}, bf16[2,128,2560]{1,2,0:T(8,128)(2,1)S(1)}, u32[]{:S(2)}, u32[]{:S(2)}) collective-permute-start(bf16[2,128,2560]{1,2,0:T(8,128)(2,1)S(1)} %collective-permute-done.6), channel_id=1, source_target_pairs={{0,16},{16,32},{32,48},{48,64},{64,80},{80,96},{96,112},{112,128},... | collective-permute-start | bytes 3932168 | tf_op jit(solution)/shard_map/ppermute | solution.py:11
  151.7 0.7 copy-start.13
  152.4 0.8 copy-start.14
  153.2 2.9 %copy-start.10 = (bf16[1,256,1024]{1,2,0:T(8,128)(2,1)S(1)}, bf16[1,256,1024]{1,2,0:T(8,128)(2,1)}, u32[]{:S(2)}) copy-start(bf16[1,256,1024]{1,2,0:T(8,128)(2,1)} %copy.178) | copy-start | bytes 1572868
where the time goes:
time: 159 us
  waiting for transfers between devices  80.9 us (51%)
  starting transfers between devices  24.7 us (16%)
  matrix products  20.4 us (13%)
  local copies, waits for them, and re-layouts  16.5 us (10%)
  other arithmetic  15 us (9%)
    ppermute x8, waiting for transfers between devices, shifted(): lax.ppermute(array, axis, [(i, (i + by) % size) for i in range(size)])  80.9 us
    ppermute x8, starting transfers between devices, shifted(): lax.ppermute(array, axis, [(i, (i + by) % size) for i in range(size)])  19.1 us
    unnamed x45, local copies, waits for them, and re-layouts  8.21 us
    dot_general x9, matrix products, attend(): jnp.einsum('qhd,khd->hqk', queries, keys.reshape(rows, heads_t, head_dim)...  6.92 us
    dot_general x9, matrix products, attend(): jnp.einsum('hqk,khd->hqd', probs.astype(jnp.bfloat16), values.reshape(row...  6.78 us
    reduce_sum x4, other arithmetic, headnorm(): jnp.mean(shaped * shaped, axis=-1, keepdims=True) + 1e-06  4.82 us
    ppermute x1, starting transfers between devices, with_halo(): lax.ppermute(lax.slice_in_dim(block, 0, width, axis=dim), axis, backward)  3.64 us
  transfers between devices with their start and end apart: 10, of which 6 were waited for; matrix products, arithmetic and copies ran while one was open for 22% of the time, Pallas kernels for 0%

commit v1 on v0

v1 whole, which is shorter than its diff:
```python
import math

import jax
import jax.numpy as jnp
from jax import lax
from jax.experimental import pallas as pl
from jax.experimental.pallas import tpu as pltpu
from jax.sharding import PartitionSpec as P

MESH = pl.DeviceIdType.MESH
BF = jnp.bfloat16
F32 = jnp.float32
REACH = 4
CH = 2
HALVES = 2
LANES = 128


def normed(x):
    return x * lax.rsqrt(jnp.mean(x * x, axis=-1, keepdims=True) + 1e-06)


def kernel(
    q_hbm, k_hbm, v_hbm, band_ref, mix_ref, lat_hbm, wqk_hbm, wv_hbm, out_hbm,
    q_in, k_in, v_in, lat, wqk, wv,
    qn, kt, qbuf, o_ref, pp, tsnd, tbuf, rsnd, rbuf, msnd, mbuf, town, sout, outv,
    in_sem, out_sem, lat_s, lat_r, q_s, q_r, t_s, t_r, r_s, r_r, m_s, m_r,
):
    az = lax.axis_index("az")
    tm = lax.axis_index("tm")
    n_az = lax.axis_size("az")
    n_tm = lax.axis_size("tm")
    heads_t, heads_s = mix_ref.shape
    rows, tokens = qn.shape[2], q_in.shape[0]
    hd = LANES
    per_half = heads_t // HALVES
    scale2 = math.log2(math.e) / math.sqrt(hd)

    def az_dev(by):
        return (lax.rem(az + by + n_az, n_az), tm)

    def tm_dev(by):
        return (az, lax.rem(tm + by + n_tm, n_tm))

    window = tokens // 2
    loads = [
        pltpu.make_async_copy(q_hbm.at[0], q_in, in_sem.at[0]),
        pltpu.make_async_copy(k_hbm.at[0], k_in, in_sem.at[1]),
        pltpu.make_async_copy(lat_hbm.at[0], lat.at[pl.ds(window, tokens)], in_sem.at[2]),
        pltpu.make_async_copy(v_hbm.at[0], v_in, in_sem.at[3]),
        pltpu.make_async_copy(wqk_hbm, wqk, in_sem.at[4]),
        pltpu.make_async_copy(wv_hbm, wv, in_sem.at[5]),
    ]
    for load in loads:
        load.start()

    barrier = pltpu.get_barrier_semaphore()
    for d in range(1, REACH + 1):
        for sign in (1, -1):
            pl.semaphore_signal(barrier, inc=1, device_id=az_dev(sign * d), device_id_type=MESH)
    for sign in (1, -1):
        pl.semaphore_signal(barrier, inc=1, device_id=tm_dev(sign), device_id_type=MESH)

    def remote(src, dst, send, recv, dev):
        return pltpu.make_async_remote_copy(
            src_ref=src, dst_ref=dst, send_sem=send, recv_sem=recv, device_id=dev, device_id_type=MESH
        )

    def q_copy(side, c, k, half):
        part = pl.ds(half * per_half, per_half)
        src = qn.at[c, part] if isinstance(k, int) and k == 1 else qbuf.at[side, c, k - 2, part]
        return remote(
            src, qbuf.at[side, c, k - 1, part],
            q_s.at[side, c, k - 1, half], q_r.at[side, c, k - 1, half], az_dev(1 - 2 * side),
        )

    def t_copy(side, c, k):
        return remote(
            tsnd.at[side, c, k - 1], tbuf.at[side, c, k - 1],
            t_s.at[side, c, k - 1], t_r.at[side, c, k - 1], az_dev((2 * side - 1) * k),
        )

    def r_copy(side, c, k):
        return remote(
            rsnd.at[c, k - 1], rbuf.at[side, c, k - 1],
            r_s.at[side, c, k - 1], r_r.at[side, c, k - 1], az_dev((1 - 2 * side) * k),
        )

    def m_copy(side, c, k):
        return remote(
            msnd.at[side, c, k - 1], mbuf.at[side, c, k - 1],
            m_s.at[side, c, k - 1], m_r.at[side, c, k - 1], az_dev(2 * side - 1),
        )

    def lat_copy(side):
        src = lat.at[pl.ds(window + (1 - side) * (tokens - window), window)]
        dst = lat.at[pl.ds(side * (tokens + window), window)]
        return remote(src, dst, lat_s.at[side], lat_r.at[side], tm_dev(1 - 2 * side))

    def norm_q(c, half):
        def one(i, _):
            h = half * per_half + i
            x = q_in[c * rows:(c + 1) * rows, pl.ds(pl.multiple_of(h * hd, hd), hd)].astype(F32)
            qn[c, h] = normed(x).astype(BF)
            return 0
        lax.fori_loop(0, per_half, one, 0, unroll=5)

    loads[0].wait()
    norm_q(0, 0)
    pl.semaphore_wait(barrier, 2 * REACH + 2)
    for side in (0, 1):
        q_copy(side, 0, 1, 0).start()
    norm_q(0, 1)
    for side in (0, 1):
        q_copy(side, 0, 1, 1).start()
    loads[2].wait()
    for side in (0, 1):
        lat_copy(side).start()
    norm_q(1, 0)
    norm_q(1, 1)

    loads[1].wait()

    def norm_k(h, _):
        x = k_in[:, pl.ds(pl.multiple_of(h * hd, hd), hd)].astype(F32)
        kt[h] = normed(x).T.astype(BF)
        return 0

    lax.fori_loop(0, heads_t, norm_k, 0, unroll=4)
    loads[3].wait()

    lane = lax.broadcasted_iota(jnp.int32, (tokens, LANES), 1)
    lane8 = lax.broadcasted_iota(jnp.int32, (8, LANES), 1)

    def scores(left, right, idx, half, sums):
        def group(i, sums):
            for j in range(5):
                h = half * per_half + i * 5 + j
                q = jnp.concatenate([left[h], right[h]], axis=0)
                s = jnp.dot(q, kt[h], preferred_element_type=F32)
                p = jnp.exp2(s * scale2)
                sums = jnp.where(lane == h, jnp.sum(p, axis=1, keepdims=True), sums)
                v = v_in[:, pl.ds(pl.multiple_of(h * hd, hd), hd)]
                o_ref[idx, h] = jnp.dot(p.astype(BF), v, preferred_element_type=F32)
            return sums
        return lax.fori_loop(0, per_half // 5, group, sums)

    half_lanes = LANES // 2

    def swap(x):
        return pltpu.roll(x, half_lanes, 1)

    def pick(x, y):
        return jnp.where(lane8 < half_lanes, x, y)

    def pack(sums):
        t = sums.T
        t0, t1, t2 = t[0:8], t[8:16], t[16:24]
        low = jnp.concatenate([pick(t0, swap(t1)), t2], axis=0)
        high = jnp.concatenate([pick(swap(t0), t1), swap(t2)], axis=0)
        return low, high

    def unpack(low, high):
        t0 = pick(low[0:8], swap(high[0:8]))
        t1 = pick(swap(low[0:8]), high[0:8])
        t2 = pick(low[8:16], swap(high[8:16]))
        return jnp.concatenate([t0, t1, t2, jnp.zeros((LANES - 24, LANES), F32)], axis=0).T

    zeros = jnp.zeros((tokens, LANES), F32)

    def own_scores():
        sums = scores(qn.at[0], qn.at[1], CH * REACH, 0, zeros)
        sums = scores(qn.at[0], qn.at[1], CH * REACH, 1, sums)
        low, high = pack(sums)
        town[0] = low
        town[1] = high

    def send_sums(c, k, sums):
        for side, t in enumerate(pack(sums)):
            tsnd[side, c, k - 1] = t.astype(BF)
            t_copy(side, c, k).start()

    def gather_sums(c):
        reach = band_ref[0, 0]
        total = town[c]
        keeps = []
        for k in range(1, REACH + 1):
            keep = jnp.where(k <= reach, 1.0, 0.0).astype(F32)
            keeps.append(keep)
            for side in (0, 1):
                t_copy(side, c, k).wait_recv()
                total = total + keep * tbuf[side, c, k - 1].astype(F32)
        inverse = 1.0 / total
        town[c] = inverse
        for k in range(1, REACH + 1):
            rsnd[c, k - 1] = (keeps[k - 1] * inverse).astype(BF)
            for side in (0, 1):
                r_copy(side, c, k).start()

    block = 32

    def mix_tile(idx, factors):
        fac_rows = factors
        town[2:] = fac_rows.reshape(tokens // 16, 16, LANES)

        def one(b, _):
            at = pl.multiple_of(b * block, block)
            f = town[pl.ds(2 + b * (block // 16), block // 16)].reshape(block, LANES)
            acc = [None] * heads_s
            for h in range(heads_t):
                x = o_ref[idx, h, pl.ds(at, block)] * f[:, h:h + 1]
                for s in range(heads_s):
                    y = x * mix_ref[h, s]
                    acc[s] = y if acc[s] is None else acc[s] + y
            for s in range(heads_s):
                pp[idx, pl.ds(at, block), s * hd:(s + 1) * hd] = acc[s]
            return 0
        lax.fori_loop(0, tokens // block, one, 0)

    def mix_remote(c, k):
        for side in (0, 1):
            r_copy(side, c, k).wait_recv()
        mix_tile(c * REACH + k - 1, unpack(rbuf[0, c, k - 1].astype(F32), rbuf[1, c, k - 1].astype(F32)))

    def pass_back(c, k):
        for side in (0, 1):
            part = pp[c * REACH + k - 1, side * rows:(side + 1) * rows]
            if k < REACH:
                m_copy(side, c, k + 1).wait_recv()
                part = part + mbuf[side, c, k].astype(F32)
            msnd[side, c, k - 1] = part.astype(BF)
            m_copy(side, c, k).start()

    span = tokens + 2 * window

    def student(pair):
        cols = 2 * hd
        at = pl.multiple_of(pair * cols, cols)
        width = heads_s * hd
        sq = jnp.dot(lat[pl.ds(window, tokens)], wqk[:, pl.ds(at, cols)], preferred_element_type=F32)
        sk = jnp.dot(lat[...], wqk[:, pl.ds(pl.multiple_of(width + pair * cols, cols), cols)], preferred_element_type=F32)
        sv = jnp.dot(lat[...], wv[:, pl.ds(at, cols)], preferred_element_type=F32).astype(BF)
        pos_q = lax.broadcasted_iota(jnp.int32, (tokens, span), 0)
        pos_k = lax.broadcasted_iota(jnp.int32, (tokens, span), 1) - window
        at_k = pos_k + tm * tokens
        keep = (jnp.abs(pos_q - pos_k) <= window) & (at_k >= 0) & (at_k < n_tm * tokens)
        for j in range(2):
            part = slice(j * hd, (j + 1) * hd)
            snq = normed(sq[:, part]).astype(BF)
            snk = normed(sk[:, part]).astype(BF)
            s = lax.dot_general(snq, snk, (((1,), (1,)), ((), ())), preferred_element_type=F32)
            p = jnp.where(keep, jnp.exp2(s * scale2), 0.0)
            total = jnp.sum(p, axis=1, keepdims=True)
            o = jnp.dot(p.astype(BF), sv[:, part], preferred_element_type=F32)
            sout[:, pl.ds(pl.multiple_of(at + j * hd, hd), hd)] = o / total

    def arrive(c, k, half, sums):
        for side in (0, 1):
            q_copy(side, c, k, half).wait_recv()
            if k < REACH:
                q_copy(side, c, k + 1, half).start()
            elif c + 1 < CH:
                q_copy(side, c + 1, 1, half).start()
        return scores(qbuf.at[0, c, k - 1], qbuf.at[1, c, k - 1], c * REACH + k - 1, half, sums)

    for k in range(1, REACH + 1):
        sums = arrive(0, k, 0, zeros)
        if k == 1:
            own_scores()
        if k == 2:
            loads[4].wait()
            loads[5].wait()
            for side in (0, 1):
                lat_copy(side).wait_recv()
        if k >= 2:
            student(k - 2)
        sums = arrive(0, k, 1, sums)
        send_sums(0, k, sums)

    for k in range(1, REACH + 1):
        sums = arrive(1, k, 0, zeros)
        if k == 1:
            student(3)
        if k == 2:
            gather_sums(0)
        if k == 4:
            mix_remote(0, 4)
            pass_back(0, 4)
        sums = arrive(1, k, 1, sums)
        send_sums(1, k, sums)
    mix_remote(0, 3)
    pass_back(0, 3)
    gather_sums(1)
    mix_remote(0, 2)
    pass_back(0, 2)
    mix_remote(1, 4)
    pass_back(1, 4)
    mix_remote(0, 1)
    pass_back(0, 1)
    mix_remote(1, 3)
    pass_back(1, 3)
    mix_remote(1, 2)
    mix_remote(1, 1)
    pass_back(1, 2)
    low, high = town[0], town[1]
    mix_tile(CH * REACH, unpack(low, high))
    pass_back(1, 1)

    for c in range(CH):
        target = pp[CH * REACH, c * rows:(c + 1) * rows]
        for side in (0, 1):
            m_copy(side, c, 1).wait_recv()
            target = target + mbuf[side, c, 0].astype(F32)
        outv[c * rows:(c + 1) * rows] = sout[c * rows:(c + 1) * rows] - target
        pltpu.make_async_copy(
            outv.at[pl.ds(c * rows, rows)], out_hbm.at[0, pl.ds(c * rows, rows)], out_sem.at[c]
        ).start()

    for side in (0, 1):
        lat_copy(side).wait_send()
        for c in range(CH):
            for k in range(1, REACH + 1):
                for half in range(HALVES):
                    q_copy(side, c, k, half).wait_send()
                t_copy(side, c, k).wait_send()
                r_copy(side, c, k).wait_send()
                m_copy(side, c, k).wait_send()
    for c in range(CH):
        pltpu.make_async_copy(
            outv.at[pl.ds(c * rows, rows)], out_hbm.at[0, pl.ds(c * rows, rows)], out_sem.at[c]
        ).wait()


def shards(teacher_q, teacher_k, teacher_v, band, head_mix, latents, w_qk, w_v):
    tokens, width = teacher_q.shape[1:]
    heads_t, heads_s = head_mix.shape
    hd = width // heads_t
    student_width = latents.shape[2]
    rows = tokens // CH
    tiles = CH * REACH
    dma = pltpu.SemaphoreType.DMA
    anywhere = pl.BlockSpec(memory_space=pl.ANY)
    scalars = pl.BlockSpec(memory_space=pltpu.SMEM)
    return pl.pallas_call(
        kernel,
        out_shape=jax.ShapeDtypeStruct((1, tokens, student_width), F32),
        in_specs=[anywhere, anywhere, anywhere, scalars, scalars, anywhere, anywhere, anywhere],
        out_specs=anywhere,
        scratch_shapes=[
            pltpu.VMEM((tokens, width), BF),
            pltpu.VMEM((tokens, width), BF),
            pltpu.VMEM((tokens, width), BF),
            pltpu.VMEM((2 * tokens, student_width), BF),
            pltpu.VMEM(w_qk.shape, BF),
            pltpu.VMEM(w_v.shape, BF),
            pltpu.VMEM((CH, heads_t, rows, hd), BF),
            pltpu.VMEM((heads_t, hd, tokens), BF),
            pltpu.VMEM((2, CH, REACH, heads_t, rows, hd), BF),
            pltpu.VMEM((tiles + 1, heads_t, tokens, hd), F32),
            pltpu.VMEM((tiles + 1, tokens, student_width), F32),
            pltpu.VMEM((2, CH, REACH, 16, LANES), BF),
            pltpu.VMEM((2, CH, REACH, 16, LANES), BF),
            pltpu.VMEM((CH, REACH, 16, LANES), BF),
            pltpu.VMEM((2, CH, REACH, 16, LANES), BF),
            pltpu.VMEM((2, CH, REACH, rows, student_width), BF),
            pltpu.VMEM((2, CH, REACH, rows, student_width), BF),
            pltpu.VMEM((2 + tokens // 16, 16, LANES), F32),
            pltpu.VMEM((tokens, student_width), F32),
            pltpu.VMEM((tokens, student_width), F32),
            dma((6,)),
            dma((CH,)),
            dma((2,)),
            dma((2,)),
            dma((2, CH, REACH, HALVES)),
            dma((2, CH, REACH, HALVES)),
            dma((2, CH, REACH)),
            dma((2, CH, REACH)),
            dma((2, CH, REACH)),
            dma((2, CH, REACH)),
            dma((2, CH, REACH)),
            dma((2, CH, REACH)),
        ],
        compiler_params=pltpu.CompilerParams(
            collective_id=0, has_side_effects=True, vmem_limit_bytes=58 * 2**20
        ),
        cost_estimate=pl.CostEstimate(flops=2 * 10**9, bytes_accessed=10**7, transcendentals=3 * 10**6),
        name="banded_teacher",
    )(teacher_q, teacher_k, teacher_v, band, head_mix, latents, w_qk, w_v)


def solution(mesh):
    in_specs = (
        P("az", "tm", None),
        P("az", "tm", None),
        P("az", "tm", None),
        P("tm", "az"),
        P(),
        P("az", "tm", None),
        P(),
        P(),
    )
    out_specs = P("az", "tm", None)
    return jax.shard_map(shards, mesh=mesh, in_specs=in_specs, out_specs=out_specs, check_vma=False)
```

time: 159 us -> 112 us (0.70)
  the two profiles are of different devices: /device:TPU:14 before, /device:TPU:8 now
where the time goes in v1:
time: 112 us
  Pallas kernels  108 us (96%)
  local copies, waits for them, and re-layouts  3.25 us (3%)
    pallas_call x1, Pallas kernels, shards(): pl.pallas_call(kernel, out_shape=jax.ShapeDtypeStruct((1, tokens, student...  108 us
    unnamed x2, local copies, waits for them, and re-layouts  3.25 us

profile of v1, /device:TPU:8, one launch (start us, length us, event | category | flops | bytes accessed | tf_op | source)
XLA Modules:
  0.0 111.8 jit_solution(10623100342634038680)
XLA Ops:
  0.7 1.4 %copy.9.mix_ref = f32[20,8]{1,0:T(8,128)} copy(f32[20,8]{0,1:T(8,128)} %param.12) | data formatting | bytes 1280 | tf_op args[4]
  2.0 107.9 %banded_teacher.1 = f32[1,128,1024]{2,1,0:T(8,128)} custom-call(bf16[1,128,2560]{2,1,0:T(8,128)(2,1)} %q_hbm.1, bf16[1,128,2560]{2,1,0:T(8,128)(2,1)} %k_hbm.1, bf16[1,128,2560]{2,1,0:T(8,128)(2,1)} %v_hbm.1, s32[1,1]{1,0:T(1,128)S(6)} %copy.11.band_ref, f32[20,8]{1,0:T(8,128)} %copy.9.mix_ref, bf16[1,128,1024]{2,1,0:T(8,128)(2,1)} %lat_hbm.1, ...), custom_call_target="tpu_custom_call" | custom-call | flops 2000000000 | bytes 10000000 | tf_op jit(solution)/shard_map/banded_teacher/pallas_call | solution.py:344
  110.0 1.9 %copy.12 = f32[1,128,1024]{2,1,0:T(8,128)} copy(f32[1,128,1024]{2,1,0:T(8,128)} %banded_teacher.1) | data formatting | bytes 1048576

commit v2 on v1

--- a/solution.py
+++ b/solution.py
@@ -12,6 +12,7 @@
 F32 = jnp.float32
 REACH = 4
 CH = 2
+PIECES = 2
 HALVES = 2
 LANES = 128
 
@@ -21,16 +22,16 @@
 
 
 def kernel(
-    q_hbm, k_hbm, v_hbm, band_ref, mix_ref, lat_hbm, wqk_hbm, wv_hbm, out_hbm,
+    q_hbm, k_hbm, v_hbm, band_ref, mix_ref, lat_hbm, wqk_hbm, wv_hbm, out_ref,
     q_in, k_in, v_in, lat, wqk, wv,
-    qn, kt, qbuf, o_ref, pp, tsnd, tbuf, rsnd, rbuf, msnd, mbuf, town, sout, outv,
-    in_sem, out_sem, lat_s, lat_r, q_s, q_r, t_s, t_r, r_s, r_r, m_s, m_r,
+    qn, kt, qbuf, o_ref, pp, tsnd, tbuf, rsnd, rbuf, msnd, mbuf, town, sout,
+    in_sem, lat_s, lat_r, q_s, q_r, t_s, t_r, r_s, r_r, m_s, m_r,
 ):
     az = lax.axis_index("az")
     tm = lax.axis_index("tm")
     n_az = lax.axis_size("az")
     n_tm = lax.axis_size("tm")
-    heads_t, heads_s = mix_ref.shape
+    heads_s, heads_t = mix_ref.shape
     rows, tokens = qn.shape[2], q_in.shape[0]
     hd = LANES
     per_half = heads_t // HALVES
@@ -43,21 +44,22 @@
         return (az, lax.rem(tm + by + n_tm, n_tm))
 
     window = tokens // 2
+    first = pl.ds(0, rows)
+    rest = pl.ds(rows, tokens - rows)
     loads = [
-        pltpu.make_async_copy(q_hbm.at[0], q_in, in_sem.at[0]),
+        pltpu.make_async_copy(q_hbm.at[0, first], q_in.at[first], in_sem.at[0]),
         pltpu.make_async_copy(k_hbm.at[0], k_in, in_sem.at[1]),
         pltpu.make_async_copy(lat_hbm.at[0], lat.at[pl.ds(window, tokens)], in_sem.at[2]),
         pltpu.make_async_copy(v_hbm.at[0], v_in, in_sem.at[3]),
         pltpu.make_async_copy(wqk_hbm, wqk, in_sem.at[4]),
         pltpu.make_async_copy(wv_hbm, wv, in_sem.at[5]),
+        pltpu.make_async_copy(q_hbm.at[0, rest], q_in.at[rest], in_sem.at[6]),
     ]
-    for load in loads:
-        load.start()
+    loads[0].start()
 
     barrier = pltpu.get_barrier_semaphore()
-    for d in range(1, REACH + 1):
-        for sign in (1, -1):
-            pl.semaphore_signal(barrier, inc=1, device_id=az_dev(sign * d), device_id_type=MESH)
+    for sign in (1, -1):
+        pl.semaphore_signal(barrier, inc=1, device_id=az_dev(sign), device_id_type=MESH)
     for sign in (1, -1):
         pl.semaphore_signal(barrier, inc=1, device_id=tm_dev(sign), device_id_type=MESH)
 
@@ -86,10 +88,13 @@
             r_s.at[side, c, k - 1], r_r.at[side, c, k - 1], az_dev((1 - 2 * side) * k),
         )
 
-    def m_copy(side, c, k):
+    piece = rows // PIECES
+
+    def m_copy(side, c, k, i):
+        part = pl.ds(i * piece, piece)
         return remote(
-            msnd.at[side, c, k - 1], mbuf.at[side, c, k - 1],
-            m_s.at[side, c, k - 1], m_r.at[side, c, k - 1], az_dev(2 * side - 1),
+            msnd.at[side, c, k - 1, part], mbuf.at[side, c, k - 1, part],
+            m_s.at[side, c, k - 1, i], m_r.at[side, c, k - 1, i], az_dev(2 * side - 1),
         )
 
     def lat_copy(side):
@@ -106,8 +111,10 @@
         lax.fori_loop(0, per_half, one, 0, unroll=5)
 
     loads[0].wait()
+    for i in (1, 2, 6, 3, 4, 5):
+        loads[i].start()
     norm_q(0, 0)
-    pl.semaphore_wait(barrier, 2 * REACH + 2)
+    pl.semaphore_wait(barrier, 4)
     for side in (0, 1):
         q_copy(side, 0, 1, 0).start()
     norm_q(0, 1)
@@ -116,9 +123,6 @@
     loads[2].wait()
     for side in (0, 1):
         lat_copy(side).start()
-    norm_q(1, 0)
-    norm_q(1, 1)
-
     loads[1].wait()
 
     def norm_k(h, _):
@@ -127,6 +131,9 @@
         return 0
 
     lax.fori_loop(0, heads_t, norm_k, 0, unroll=4)
+    loads[6].wait()
+    norm_q(1, 0)
+    norm_q(1, 1)
     loads[3].wait()
 
     lane = lax.broadcasted_iota(jnp.int32, (tokens, LANES), 1)
@@ -210,7 +217,7 @@
             for h in range(heads_t):
                 x = o_ref[idx, h, pl.ds(at, block)] * f[:, h:h + 1]
                 for s in range(heads_s):
-                    y = x * mix_ref[h, s]
+                    y = x * mix_ref[s, h]
                     acc[s] = y if acc[s] is None else acc[s] + y
             for s in range(heads_s):
                 pp[idx, pl.ds(at, block), s * hd:(s + 1) * hd] = acc[s]
@@ -223,13 +230,15 @@
         mix_tile(c * REACH + k - 1, unpack(rbuf[0, c, k - 1].astype(F32), rbuf[1, c, k - 1].astype(F32)))
 
     def pass_back(c, k):
-        for side in (0, 1):
-            part = pp[c * REACH + k - 1, side * rows:(side + 1) * rows]
-            if k < REACH:
-                m_copy(side, c, k + 1).wait_recv()
-                part = part + mbuf[side, c, k].astype(F32)
-            msnd[side, c, k - 1] = part.astype(BF)
-            m_copy(side, c, k).start()
+        for i in range(PIECES):
+            at = slice(i * piece, (i + 1) * piece)
+            for side in (0, 1):
+                part = pp[c * REACH + k - 1, side * rows + i * piece:side * rows + (i + 1) * piece]
+                if k < REACH:
+                    m_copy(side, c, k + 1, i).wait_recv()
+                    part = part + mbuf[side, c, k, at].astype(F32)
+                msnd[side, c, k - 1, at] = part.astype(BF)
+                m_copy(side, c, k, i).start()
 
     span = tokens + 2 * window
 
@@ -283,38 +292,33 @@
             student(3)
         if k == 2:
             gather_sums(0)
+        if k == 3:
+            mix_remote(0, 4)
         if k == 4:
-            mix_remote(0, 4)
             pass_back(0, 4)
+            mix_remote(0, 2)
         sums = arrive(1, k, 1, sums)
         send_sums(1, k, sums)
-    mix_remote(0, 3)
+        if k == 3:
+            mix_remote(0, 3)
     pass_back(0, 3)
+    mix_remote(0, 1)
+    pass_back(0, 2)
     gather_sums(1)
-    mix_remote(0, 2)
-    pass_back(0, 2)
-    mix_remote(1, 4)
-    pass_back(1, 4)
-    mix_remote(0, 1)
     pass_back(0, 1)
-    mix_remote(1, 3)
-    pass_back(1, 3)
-    mix_remote(1, 2)
-    mix_remote(1, 1)
-    pass_back(1, 2)
-    low, high = town[0], town[1]
-    mix_tile(CH * REACH, unpack(low, high))
-    pass_back(1, 1)
+    mix_tile(CH * REACH, unpack(town[0], town[1]))
+    for k in range(REACH, 0, -1):
+        mix_remote(1, k)
+        pass_back(1, k)
 
     for c in range(CH):
-        target = pp[CH * REACH, c * rows:(c + 1) * rows]
-        for side in (0, 1):
-            m_copy(side, c, 1).wait_recv()
-            target = target + mbuf[side, c, 0].astype(F32)
-        outv[c * rows:(c + 1) * rows] = sout[c * rows:(c + 1) * rows] - target
-        pltpu.make_async_copy(
-            outv.at[pl.ds(c * rows, rows)], out_hbm.at[0, pl.ds(c * rows, rows)], out_sem.at[c]
-        ).start()
+        for i in range(PIECES):
+            at = slice(c * rows + i * piece, c * rows + (i + 1) * piece)
+            target = pp[CH * REACH, at]
+            for side in (0, 1):
+                m_copy(side, c, 1, i).wait_recv()
+                target = target + mbuf[side, c, 0, i * piece:(i + 1) * piece].astype(F32)
+            out_ref[0, at] = sout[at] - target
 
     for side in (0, 1):
         lat_copy(side).wait_send()
@@ -324,11 +328,8 @@
                     q_copy(side, c, k, half).wait_send()
                 t_copy(side, c, k).wait_send()
                 r_copy(side, c, k).wait_send()
-                m_copy(side, c, k).wait_send()
-    for c in range(CH):
-        pltpu.make_async_copy(
-            outv.at[pl.ds(c * rows, rows)], out_hbm.at[0, pl.ds(c * rows, rows)], out_sem.at[c]
-        ).wait()
+                for i in range(PIECES):
+                    m_copy(side, c, k, i).wait_send()
 
 
 def shards(teacher_q, teacher_k, teacher_v, band, head_mix, latents, w_qk, w_v):
@@ -343,9 +344,9 @@
     scalars = pl.BlockSpec(memory_space=pltpu.SMEM)
     return pl.pallas_call(
         kernel,
-        out_shape=jax.ShapeDtypeStruct((1, tokens, student_width), F32),
+        out_shape=pltpu.VMEM((1, tokens, student_width), F32),
         in_specs=[anywhere, anywhere, anywhere, scalars, scalars, anywhere, anywhere, anywhere],
-        out_specs=anywhere,
+        out_specs=pl.BlockSpec(memory_space=pltpu.VMEM),
         scratch_shapes=[
             pltpu.VMEM((tokens, width), BF),
             pltpu.VMEM((tokens, width), BF),
@@ -366,9 +367,7 @@
             pltpu.VMEM((2, CH, REACH, rows, student_width), BF),
             pltpu.VMEM((2 + tokens // 16, 16, LANES), F32),
             pltpu.VMEM((tokens, student_width), F32),
-            pltpu.VMEM((tokens, student_width), F32),
-            dma((6,)),
-            dma((CH,)),
+            dma((7,)),
             dma((2,)),
             dma((2,)),
             dma((2, CH, REACH, HALVES)),
@@ -377,15 +376,15 @@
             dma((2, CH, REACH)),
             dma((2, CH, REACH)),
             dma((2, CH, REACH)),
-            dma((2, CH, REACH)),
-            dma((2, CH, REACH)),
+            dma((2, CH, REACH, PIECES)),
+            dma((2, CH, REACH, PIECES)),
         ],
         compiler_params=pltpu.CompilerParams(
-            collective_id=0, has_side_effects=True, vmem_limit_bytes=58 * 2**20
+            collective_id=0, has_side_effects=True, vmem_limit_bytes=56 * 2**20
         ),
         cost_estimate=pl.CostEstimate(flops=2 * 10**9, bytes_accessed=10**7, transcendentals=3 * 10**6),
         name="banded_teacher",
-    )(teacher_q, teacher_k, teacher_v, band, head_mix, latents, w_qk, w_v)
+    )(teacher_q, teacher_k, teacher_v, band, head_mix.T, latents, w_qk, w_v)
 
 
 def solution(mesh):

time: 112 us -> 108 us (0.964)
  local copies, waits for them, and re-layouts: 3.25 us -> 0.8 us
  Pallas kernels: 108 us -> 106 us
    unnamed x2 -> x1, local copies, waits for them, and re-layouts: 3.25 us -> 0.8 us
    pallas_call x1, Pallas kernels: 108 us -> 106 us  [shards(): pl.pallas_call(kernel, out_shape=pltpu.VMEM((1, tokens, student_width), F...]
where the time goes in v2:
time: 108 us
  Pallas kernels  106 us (98%)
    pallas_call x1, Pallas kernels, shards(): pl.pallas_call(kernel, out_shape=pltpu.VMEM((1, tokens, student_width), F...  106 us

profile of v2, /device:TPU:8, one launch (start us, length us, event | category | flops | bytes accessed | tf_op | source)
XLA Modules:
  0.0 107.5 jit_solution(14913118248457346642)
XLA Ops:
  0.7 106.1 %banded_teacher.1 = f32[1,128,1024]{2,1,0:T(8,128)S(1)} custom-call(bf16[1,128,2560]{2,1,0:T(8,128)(2,1)} %q_hbm.1, bf16[1,128,2560]{2,1,0:T(8,128)(2,1)} %k_hbm.1, bf16[1,128,2560]{2,1,0:T(8,128)(2,1)} %v_hbm.1, s32[1,1]{1,0:T(1,128)S(6)} %copy.11.band_ref, f32[8,20]{1,0:T(8,128)} %bitcast.1, bf16[1,128,1024]{2,1,0:T(8,128)(2,1)} %lat_hbm.1, ...), custom_call_target="tpu_custom_call" | custom-call | flops 2000000000 | bytes 10000000 | tf_op jit(solution)/shard_map/banded_teacher/pallas_call | solution.py:345
  106.7 0.8 copy.10

commit v3 on v2

v3 whole, which is shorter than its diff:
```python
import math

import jax
import jax.numpy as jnp
from jax import lax
from jax.experimental import pallas as pl
from jax.experimental.pallas import tpu as pltpu
from jax.sharding import PartitionSpec as P

MESH = pl.DeviceIdType.MESH
BF = jnp.bfloat16
F32 = jnp.float32
REACH = 4
SPLIT = (96, 32)
PIECE = (32, 16)
CH = len(SPLIT)
START = (0, 96)
PIECES = tuple(n // p for n, p in zip(SPLIT, PIECE))
PARTS = (4, 2)
LANES = 128


def normed(x):
    return x * lax.rsqrt(jnp.mean(x * x, axis=-1, keepdims=True) + 1e-06)


def kernel(
    q_hbm, k_hbm, v_hbm, band_ref, mix_ref, lat_hbm, wqk_hbm, wv_hbm, out_ref,
    q_in, k_in, v_in, lat, wqk, wv,
    qn0, qn1, kt, qbuf0, qbuf1, o0, o1, o_own, pp0, pp1, pp_own, tsnd, tbuf, rsnd, rbuf,
    msnd0, msnd1, mbuf0, mbuf1, abuf, town, fac, sout,
    in_sem, lat_s, lat_r, q_s, q_r, t_s, t_r, r_s, r_r, m_s, m_r, a_s, a_r,
):
    az = lax.axis_index("az")
    tm = lax.axis_index("tm")
    n_az = lax.axis_size("az")
    n_tm = lax.axis_size("tm")
    heads_s, heads_t = mix_ref.shape
    tokens = q_in.shape[0]
    qn, qbuf, o_ref, pp = (qn0, qn1), (qbuf0, qbuf1), (o0, o1), (pp0, pp1)
    msnd, mbuf = (msnd0, msnd1), (mbuf0, mbuf1)
    hd = LANES
    heads_in = [heads_t // n for n in PARTS]
    scale2 = math.log2(math.e) / math.sqrt(hd)

    def az_dev(by):
        return (lax.rem(az + by + n_az, n_az), tm)

    def tm_dev(by):
        return (az, lax.rem(tm + by + n_tm, n_tm))

    window = tokens // 2
    first = pl.ds(0, SPLIT[0])
    rest = pl.ds(SPLIT[0], SPLIT[1])
    loads = [
        pltpu.make_async_copy(q_hbm.at[0, first], q_in.at[first], in_sem.at[0]),
        pltpu.make_async_copy(k_hbm.at[0], k_in, in_sem.at[1]),
        pltpu.make_async_copy(lat_hbm.at[0], lat.at[pl.ds(window, tokens)], in_sem.at[2]),
        pltpu.make_async_copy(v_hbm.at[0], v_in, in_sem.at[3]),
        pltpu.make_async_copy(wqk_hbm, wqk, in_sem.at[4]),
        pltpu.make_async_copy(wv_hbm, wv, in_sem.at[5]),
        pltpu.make_async_copy(q_hbm.at[0, rest], q_in.at[rest], in_sem.at[6]),
    ]
    loads[0].start()
    to_right, to_left = tm < n_tm - 1, tm > 0

    @pl.when(tm == 0)
    def _():
        lat[0:window] = jnp.zeros((window, lat.shape[1]), BF)

    @pl.when(tm == n_tm - 1)
    def _():
        lat[tokens + window:] = jnp.zeros((window, lat.shape[1]), BF)


    barrier = pltpu.get_barrier_semaphore()
    for sign in (1, -1):
        pl.semaphore_signal(barrier, inc=1, device_id=az_dev(sign), device_id_type=MESH)
    for sign in (1, -1):
        pl.semaphore_signal(barrier, inc=1, device_id=tm_dev(sign), device_id_type=MESH)

    def remote(src, dst, send, recv, dev):
        return pltpu.make_async_remote_copy(
            src_ref=src, dst_ref=dst, send_sem=send, recv_sem=recv, device_id=dev, device_id_type=MESH
        )

    def q_copy(side, c, k, i):
        part = pl.ds(i * heads_in[c], heads_in[c])
        src = qn[c].at[part] if k == 1 else qbuf[c].at[side, k - 2, part]
        return remote(
            src, qbuf[c].at[side, k - 1, part],
            q_s.at[side, c, k - 1, i], q_r.at[side, c, k - 1, i], az_dev(1 - 2 * side),
        )

    def t_copy(side, c, k):
        return remote(
            tsnd.at[side, c, k - 1], tbuf.at[side, c, k - 1],
            t_s.at[side, c, k - 1], t_r.at[side, c, k - 1], az_dev((2 * side - 1) * k),
        )

    def r_copy(side, c, k):
        return remote(
            rsnd.at[c, k - 1], rbuf.at[side, c, k - 1],
            r_s.at[side, c, k - 1], r_r.at[side, c, k - 1], az_dev((1 - 2 * side) * k),
        )

    def a_copy(side):
        last = CH - 1
        return remote(
            tsnd.at[side, last, REACH - 1], abuf.at[1 - side], a_s.at[side], a_r.at[1 - side], az_dev(2 * REACH)
        )

    def m_copy(side, c, k, i):
        part = pl.ds(i * PIECE[c], PIECE[c])
        return remote(
            msnd[c].at[side, k - 1, part], mbuf[c].at[side, k - 1, part],
            m_s.at[side, c, k - 1, i], m_r.at[side, c, k - 1, i], az_dev(2 * side - 1),
        )

    def lat_copy(side):
        src = lat.at[pl.ds(window + (1 - side) * (tokens - window), window)]
        dst = lat.at[pl.ds(side * (tokens + window), window)]
        return remote(src, dst, lat_s.at[side], lat_r.at[side], tm_dev(1 - 2 * side))

    def norm_q(c, i):
        def one(j, _):
            h = i * heads_in[c] + j
            x = q_in[START[c]:START[c] + SPLIT[c], pl.ds(pl.multiple_of(h * hd, hd), hd)].astype(F32)
            qn[c][h] = normed(x).astype(BF)
            return 0
        lax.fori_loop(0, heads_in[c], one, 0, unroll=5)

    def norm_k(h, _):
        x = k_in[:, pl.ds(pl.multiple_of(h * hd, hd), hd)].astype(F32)
        kt[h] = normed(x).T.astype(BF)
        return 0

    def send_first(c, i):
        for side in (0, 1):
            q_copy(side, c, 1, i).start()

    loads[0].wait()
    for i in (1, 2, 6, 3, 4, 5):
        loads[i].start()
    norm_q(0, 0)
    pl.semaphore_wait(barrier, 4)
    send_first(0, 0)
    for i in range(1, PARTS[0]):
        norm_q(0, i)
    loads[1].wait()
    lax.fori_loop(0, heads_t // 2, norm_k, 0, unroll=5)
    send_first(0, 1)
    lax.fori_loop(heads_t // 2, heads_t, norm_k, 0, unroll=5)
    send_first(0, 2)
    loads[6].wait()
    for i in range(PARTS[1]):
        norm_q(1, i)
    loads[2].wait()
    pl.when(to_right)(lat_copy(0).start)
    pl.when(to_left)(lat_copy(1).start)
    loads[3].wait()
    send_first(0, 3)

    lane8 = lax.broadcasted_iota(jnp.int32, (8, LANES), 1)
    row8 = lax.broadcasted_iota(jnp.int32, (8, LANES), 0)

    def scores(left, right, dst, first, count, sums):
        lane = lax.broadcasted_iota(jnp.int32, sums.shape, 1)

        def group(i, sums):
            for j in range(5):
                h = first + i * 5 + j
                q = jnp.concatenate([left[h], right[h]], axis=0)
                s = jnp.dot(q, kt[h], preferred_element_type=F32)
                p = jnp.exp2(s * scale2)
                sums = jnp.where(lane == h, jnp.sum(p, axis=1, keepdims=True), sums)
                v = v_in[:, pl.ds(pl.multiple_of(h * hd, hd), hd)]
                dst[h] = jnp.dot(p.astype(BF), v, preferred_element_type=F32)
            return sums
        return lax.fori_loop(0, count // 5, group, sums)

    def roll(x, by):
        return pltpu.roll(x, by, 1)

    def lift(x):
        return pltpu.roll(x, 4, 0)

    def below(n, x, y):
        return jnp.where(lane8 < n, x, y)

    def by_head(x):
        if x.shape[0] < LANES:
            x = jnp.concatenate([x, jnp.zeros((LANES - x.shape[0], LANES), F32)], axis=0)
        t = x.T
        return t[0:8], t[8:16], t[16:24]

    def by_query(t0, t1, t2):
        return jnp.concatenate([t0, t1, t2, jnp.zeros((LANES - 24, LANES), F32)], axis=0).T

    def pack_large(t):
        t0, t1, t2 = t
        tail = jnp.where(row8 < 4, roll(t2, 96), lift(roll(t2, 64)))
        return jnp.concatenate([below(96, t0, tail), below(96, t1, roll(t2, 32))], axis=0)

    def unpack_large(x):
        m0, m1 = x[0:8], x[8:16]
        return m0, m1, below(32, roll(m0, 32), below(64, lift(roll(m0, 64)), roll(m1, 96)))

    def pack_small(t, at):
        def to(x, lanes):
            by = (lanes - at) % LANES
            return roll(x, by) if by else x
        m = below(32, to(t[0], 0), below(64, to(t[1], 32), to(t[2], 64)))
        return jnp.concatenate([m, jnp.zeros((8, LANES), F32)], axis=0)

    def unpack_small(x, at):
        m = x[0:8]

        def to(lanes):
            by = (at - lanes) % LANES
            return roll(m, by) if by else m
        return to(0), to(32), to(64)

    def pack(c, sums):
        n = SPLIT[c]
        if c == 0:
            return pack_large(by_head(sums[0:n])), pack_large(by_head(sums[n:2 * n]))
        t = by_head(sums)
        return pack_small(t, 0), pack_small(t, n)

    def unpack(c, left, right):
        n = SPLIT[c]
        if c == 0:
            return jnp.concatenate([by_query(*unpack_large(x))[0:n] for x in (left, right)], axis=0)
        both = zip(unpack_small(left, 0), unpack_small(right, n))
        return by_query(*[below(n, x, y) for x, y in both])[0:2 * n]

    def own_scores():
        sums = scores(qn[0], qn[1], o_own, 0, heads_t, jnp.zeros((tokens, LANES), F32))
        t = by_head(sums)
        town[0] = pack_large(t)
        town[1] = pack_small(t, START[1])

    def send_sums(c, k, sums):
        for side, t in enumerate(pack(c, sums)):
            tsnd[side, c, k - 1] = t.astype(BF)
            if c == CH - 1 and k == REACH:
                a_copy(side).start()
            t_copy(side, c, k).start()

    reach = band_ref[0, 0]

    def within(k):
        return jnp.where(k <= reach, 1.0, 0.0).astype(F32)

    def add_sums(c, total, ks):
        for k in ks:
            for side in (0, 1):
                t_copy(side, c, k).wait_recv()
                total = total + within(k) * tbuf[side, c, k - 1].astype(F32)
        return total

    def send_factors(c, k, value):
        rsnd[c, k - 1] = value.astype(BF)
        for side in (0, 1):
            r_copy(side, c, k).start()

    def gather_sums(c):
        inverse = 1.0 / add_sums(c, town[c], range(1, REACH + 1))
        town[c] = inverse
        for k in range(REACH, 0, -1):
            send_factors(c, k, within(k) * inverse)

    def gather_near():
        c = CH - 1
        total = add_sums(c, town[c], range(1, REACH))
        town[c] = total
        send_factors(c, REACH, jnp.where(jnp.full(total.shape, reach) >= REACH, total, jnp.inf))

    def gather_far():
        c = CH - 1
        inverse = 1.0 / add_sums(c, town[c], (REACH,))
        town[c] = inverse
        for k in range(REACH - 1, 0, -1):
            send_factors(c, k, within(k) * inverse)

    block = 32

    def mix_tile(o, dst, factors):
        n = factors.shape[0]
        fac[0:n] = factors

        def one(b, _):
            at = pl.ds(pl.multiple_of(b * block, block), block)
            f = fac[at]
            acc = [None] * heads_s
            for h in range(heads_t):
                x = o[h, at] * f[:, h:h + 1]
                for s in range(heads_s):
                    y = x * mix_ref[s, h]
                    acc[s] = y if acc[s] is None else acc[s] + y
            for s in range(heads_s):
                dst[at, s * hd:(s + 1) * hd] = acc[s]
            return 0
        lax.fori_loop(0, n // block, one, 0)

    def mix_remote(c, k):
        for side in (0, 1):
            r_copy(side, c, k).wait_recv()
        sent = [rbuf[side, c, k - 1].astype(F32) for side in (0, 1)]
        if c == CH - 1 and k == REACH:
            for side in (0, 1):
                a_copy(1 - side).wait_recv()
                sent[side] = 1.0 / (sent[side] + tsnd[side, c, k - 1].astype(F32) + abuf[side].astype(F32))
        factors = unpack(c, *sent)
        mix_tile(o_ref[c].at[k - 1], pp[c].at[k - 1], factors)

    def mix_own():
        large = unpack_large(town[0])
        small = unpack_small(town[1], START[1])
        mix_tile(o_own, pp_own, by_query(*[below(START[1], x, y) for x, y in zip(large, small)]))

    def pass_back(c, k, pieces=None):
        for i in range(PIECES[c]) if pieces is None else pieces:
            at = slice(i * PIECE[c], (i + 1) * PIECE[c])
            for side in (0, 1):
                share = side * SPLIT[c] + i * PIECE[c]
                part = pp[c][k - 1, share:share + PIECE[c]]
                if k < REACH:
                    m_copy(side, c, k + 1, i).wait_recv()
                    part = part + mbuf[c][side, k, at].astype(F32)
                msnd[c][side, k - 1, at] = part.astype(BF)
                m_copy(side, c, k, i).start()

    span = tokens + 2 * window

    def student(pair):
        cols = 2 * hd
        at = pl.multiple_of(pair * cols, cols)
        width = heads_s * hd
        sq = jnp.dot(lat[pl.ds(window, tokens)], wqk[:, pl.ds(at, cols)], preferred_element_type=F32)
        sk = jnp.dot(lat[...], wqk[:, pl.ds(pl.multiple_of(width + pair * cols, cols), cols)], preferred_element_type=F32)
        sv = jnp.dot(lat[...], wv[:, pl.ds(at, cols)], preferred_element_type=F32).astype(BF)
        pos_q = lax.broadcasted_iota(jnp.int32, (tokens, span), 0)
        pos_k = lax.broadcasted_iota(jnp.int32, (tokens, span), 1) - window
        at_k = pos_k + tm * tokens
        keep = (jnp.abs(pos_q - pos_k) <= window) & (at_k >= 0) & (at_k < n_tm * tokens)
        for j in range(2):
            part = slice(j * hd, (j + 1) * hd)
            snq = normed(sq[:, part]).astype(BF)
            snk = normed(sk[:, part]).astype(BF)
            s = lax.dot_general(snq, snk, (((1,), (1,)), ((), ())), preferred_element_type=F32)
            p = jnp.where(keep, jnp.exp2(s * scale2), 0.0)
            total = jnp.sum(p, axis=1, keepdims=True)
            o = jnp.dot(p.astype(BF), sv[:, part], preferred_element_type=F32)
            sout[:, pl.ds(pl.multiple_of(at + j * hd, hd), hd)] = o / total

    def arrive(c, k, i, sums):
        for side in (0, 1):
            q_copy(side, c, k, i).wait_recv()
            if k < REACH:
                q_copy(side, c, k + 1, i).start()
        if k == REACH and c + 1 < CH:
            for n in range(PARTS[c + 1]):
                if (n + 1) * PARTS[c] // PARTS[c + 1] - 1 == i:
                    send_first(c + 1, n)
        if sums is None:
            sums = jnp.zeros((2 * SPLIT[c], LANES), F32)
        return scores(qbuf[c].at[0, k - 1], qbuf[c].at[1, k - 1], o_ref[c].at[k - 1], i * heads_in[c], heads_in[c], sums)

    own_scores()
    for k in range(1, REACH + 1):
        sums = None
        for i in range(PARTS[0]):
            sums = arrive(0, k, i, sums)
            if k == 1 and i == 1:
                loads[4].wait()
                loads[5].wait()
                pl.when(to_left)(lat_copy(0).wait_recv)
                pl.when(to_right)(lat_copy(1).wait_recv)
            if i == 2:
                student(k - 1)
        send_sums(0, k, sums)

    for k in range(1, REACH + 1):
        sums = arrive(1, k, 0, None)
        if k == 2:
            gather_sums(0)
        sums = arrive(1, k, 1, sums)
        send_sums(1, k, sums)
        if k == 3:
            mix_remote(0, 4)
            pass_back(0, 4)
            mix_remote(0, 3)
    gather_near()
    pass_back(0, 3)
    gather_far()
    mix_remote(1, 4)
    pass_back(1, 4)
    mix_remote(0, 2)
    pass_back(0, 2)
    mix_remote(1, 3)
    pass_back(1, 3)
    mix_remote(0, 1)
    pass_back(0, 1)
    mix_remote(1, 2)
    pass_back(1, 2)
    mix_remote(1, 1)
    mix_own()
    pass_back(1, 1)

    for c in range(CH):
        for i in range(PIECES[c]):
            at = slice(START[c] + i * PIECE[c], START[c] + (i + 1) * PIECE[c])
            target = pp_own[at]
            for side in (0, 1):
                m_copy(side, c, 1, i).wait_recv()
                target = target + mbuf[c][side, 0, i * PIECE[c]:(i + 1) * PIECE[c]].astype(F32)
            out_ref[0, at] = sout[at] - target

    pl.when(to_right)(lat_copy(0).wait_send)
    pl.when(to_left)(lat_copy(1).wait_send)
    for side in (0, 1):
        a_copy(side).wait_send()
        for c in range(CH):
            for k in range(1, REACH + 1):
                for i in range(PARTS[c]):
                    q_copy(side, c, k, i).wait_send()
                t_copy(side, c, k).wait_send()
                r_copy(side, c, k).wait_send()
                for i in range(PIECES[c]):
                    m_copy(side, c, k, i).wait_send()


def shards(teacher_q, teacher_k, teacher_v, band, head_mix, latents, w_qk, w_v):
    tokens, width = teacher_q.shape[1:]
    heads_t, heads_s = head_mix.shape
    hd = width // heads_t
    student_width = latents.shape[2]
    dma = pltpu.SemaphoreType.DMA
    anywhere = pl.BlockSpec(memory_space=pl.ANY)
    scalars = pl.BlockSpec(memory_space=pltpu.SMEM)
    return pl.pallas_call(
        kernel,
        out_shape=pltpu.VMEM((1, tokens, student_width), F32),
        in_specs=[anywhere, anywhere, anywhere, scalars, scalars, anywhere, anywhere, anywhere],
        out_specs=pl.BlockSpec(memory_space=pltpu.VMEM),
        scratch_shapes=[
            pltpu.VMEM((tokens, width), BF),
            pltpu.VMEM((tokens, width), BF),
            pltpu.VMEM((tokens, width), BF),
            pltpu.VMEM((2 * tokens, student_width), BF),
            pltpu.VMEM(w_qk.shape, BF),
            pltpu.VMEM(w_v.shape, BF),
            *[pltpu.VMEM((heads_t, n, hd), BF) for n in SPLIT],
            pltpu.VMEM((heads_t, hd, tokens), BF),
            *[pltpu.VMEM((2, REACH, heads_t, n, hd), BF) for n in SPLIT],
            *[pltpu.VMEM((REACH, heads_t, 2 * n, hd), F32) for n in SPLIT],
            pltpu.VMEM((heads_t, tokens, hd), F32),
            *[pltpu.VMEM((REACH, 2 * n, student_width), F32) for n in SPLIT],
            pltpu.VMEM((tokens, student_width), F32),
            pltpu.VMEM((2, CH, REACH, 16, LANES), BF),
            pltpu.VMEM((2, CH, REACH, 16, LANES), BF),
            pltpu.VMEM((CH, REACH, 16, LANES), BF),
            pltpu.VMEM((2, CH, REACH, 16, LANES), BF),
            *[pltpu.VMEM((2, REACH, n, student_width), BF) for n in SPLIT],
            *[pltpu.VMEM((2, REACH, n, student_width), BF) for n in SPLIT],
            pltpu.VMEM((2, 16, LANES), BF),
            pltpu.VMEM((CH, 16, LANES), F32),
            pltpu.VMEM((2 * max(SPLIT), LANES), F32),
            pltpu.VMEM((tokens, student_width), F32),
            dma((7,)),
            dma((2,)),
            dma((2,)),
            dma((2, CH, REACH, max(PARTS))),
            dma((2, CH, REACH, max(PARTS))),
            dma((2, CH, REACH)),
            dma((2, CH, REACH)),
            dma((2, CH, REACH)),
            dma((2, CH, REACH)),
            dma((2, CH, REACH, max(PIECES))),
            dma((2, CH, REACH, max(PIECES))),
            dma((2,)),
            dma((2,)),
        ],
        compiler_params=pltpu.CompilerParams(
            collective_id=0, has_side_effects=True, vmem_limit_bytes=56 * 2**20
        ),
        cost_estimate=pl.CostEstimate(flops=2 * 10**9, bytes_accessed=10**7, transcendentals=3 * 10**6),
        name="banded_teacher",
    )(teacher_q, teacher_k, teacher_v, band, head_mix.T, latents, w_qk, w_v)


def solution(mesh):
    in_specs = (
        P("az", "tm", None),
        P("az", "tm", None),
        P("az", "tm", None),
        P("tm", "az"),
        P(),
        P("az", "tm", None),
        P(),
        P(),
    )
    out_specs = P("az", "tm", None)
    return jax.shard_map(shards, mesh=mesh, in_specs=in_specs, out_specs=out_specs, check_vma=False)
```

time: 108 us -> 104 us (0.963)
  Pallas kernels: 106 us -> 101 us
    pallas_call x1, Pallas kernels: 106 us -> 101 us  [shards(): pl.pallas_call(kernel, out_shape=pltpu.VMEM((1, tokens, student_width), F...]
where the time goes in v3:
time: 104 us; the launch traced here: 102 us
  Pallas kernels  101 us (97%)
    pallas_call x1, Pallas kernels, shards(): pl.pallas_call(kernel, out_shape=pltpu.VMEM((1, tokens, student_width), F...  101 us

profile of v3, /device:TPU:8, one launch (start us, length us, event | category | flops | bytes accessed | tf_op | source)
XLA Modules:
  0.0 102.5 jit_solution(11599177744081492465)
XLA Ops:
  0.7 101.0 %banded_teacher.1 = f32[1,128,1024]{2,1,0:T(8,128)S(1)} custom-call(bf16[1,128,2560]{2,1,0:T(8,128)(2,1)} %q_hbm.1, bf16[1,128,2560]{2,1,0:T(8,128)(2,1)} %k_hbm.1, bf16[1,128,2560]{2,1,0:T(8,128)(2,1)} %v_hbm.1, s32[1,1]{1,0:T(1,128)S(6)} %copy.11.band_ref, f32[8,20]{1,0:T(8,128)} %bitcast.1, bf16[1,128,1024]{2,1,0:T(8,128)(2,1)} %lat_hbm.1, ...), custom_call_target="tpu_custom_call" | custom-call | flops 2000000000 | bytes 10000000 | tf_op jit(solution)/shard_map/banded_teacher/pallas_call | solution.py:443
  101.7 0.8 copy.10

commit v4 on v3

--- a/solution.py
+++ b/solution.py
@@ -76,8 +76,10 @@
     barrier = pltpu.get_barrier_semaphore()
     for sign in (1, -1):
         pl.semaphore_signal(barrier, inc=1, device_id=az_dev(sign), device_id_type=MESH)
-    for sign in (1, -1):
-        pl.semaphore_signal(barrier, inc=1, device_id=tm_dev(sign), device_id_type=MESH)
+    for sign, there in ((1, to_right), (-1, to_left)):
+        @pl.when(there)
+        def _(sign=sign):
+            pl.semaphore_signal(barrier, inc=1, device_id=tm_dev(sign), device_id_type=MESH)
 
     def remote(src, dst, send, recv, dev):
         return pltpu.make_async_remote_copy(
@@ -143,7 +145,7 @@
     for i in (1, 2, 6, 3, 4, 5):
         loads[i].start()
     norm_q(0, 0)
-    pl.semaphore_wait(barrier, 4)
+    pl.semaphore_wait(barrier, 2 + lax.min(tm, 1) + lax.min(n_tm - 1 - tm, 1))
     send_first(0, 0)
     for i in range(1, PARTS[0]):
         norm_q(0, i)
@@ -402,21 +404,13 @@
     mix_remote(1, 3)
     pass_back(1, 3)
     mix_remote(0, 1)
-    pass_back(0, 1)
     mix_remote(1, 2)
+    pass_back(0, 1, (0,))
     pass_back(1, 2)
+    pass_back(0, 1, (1, 2))
     mix_remote(1, 1)
     mix_own()
     pass_back(1, 1)
-
-    for c in range(CH):
-        for i in range(PIECES[c]):
-            at = slice(START[c] + i * PIECE[c], START[c] + (i + 1) * PIECE[c])
-            target = pp_own[at]
-            for side in (0, 1):
-                m_copy(side, c, 1, i).wait_recv()
-                target = target + mbuf[c][side, 0, i * PIECE[c]:(i + 1) * PIECE[c]].astype(F32)
-            out_ref[0, at] = sout[at] - target
 
     pl.when(to_right)(lat_copy(0).wait_send)
     pl.when(to_left)(lat_copy(1).wait_send)
@@ -428,8 +422,23 @@
                     q_copy(side, c, k, i).wait_send()
                 t_copy(side, c, k).wait_send()
                 r_copy(side, c, k).wait_send()
-                for i in range(PIECES[c]):
-                    m_copy(side, c, k, i).wait_send()
+                if k > 1:
+                    for i in range(PIECES[c]):
+                        m_copy(side, c, k, i).wait_send()
+
+    for c in range(CH):
+        for i in range(PIECES[c]):
+            at = slice(START[c] + i * PIECE[c], START[c] + (i + 1) * PIECE[c])
+            target = pp_own[at]
+            for side in (0, 1):
+                m_copy(side, c, 1, i).wait_recv()
+                target = target + mbuf[c][side, 0, i * PIECE[c]:(i + 1) * PIECE[c]].astype(F32)
+            out_ref[0, at] = sout[at] - target
+
+    for side in (0, 1):
+        for c in range(CH):
+            for i in range(PIECES[c]):
+                m_copy(side, c, 1, i).wait_send()
 
 
 def shards(teacher_q, teacher_k, teacher_v, band, head_mix, latents, w_qk, w_v):

time: 104 us -> 103 us (level)
  no operation moved by 1% of the time
where the time goes in v4:
time: 103 us; the launch traced here: 102 us
  Pallas kernels  100 us (97%)
    pallas_call x1, Pallas kernels, shards(): pl.pallas_call(kernel, out_shape=pltpu.VMEM((1, tokens, student_width), F...  100 us

profile of v4, /device:TPU:8, one launch (start us, length us, event | category | flops | bytes accessed | tf_op | source)
XLA Modules:
  0.0 101.7 jit_solution(3841904716015043199)
XLA Ops:
  0.7 100.2 %banded_teacher.1 = f32[1,128,1024]{2,1,0:T(8,128)S(1)} custom-call(bf16[1,128,2560]{2,1,0:T(8,128)(2,1)} %q_hbm.1, bf16[1,128,2560]{2,1,0:T(8,128)(2,1)} %k_hbm.1, bf16[1,128,2560]{2,1,0:T(8,128)(2,1)} %v_hbm.1, s32[1,1]{1,0:T(1,128)S(6)} %copy.11.band_ref, f32[8,20]{1,0:T(8,128)} %bitcast.1, bf16[1,128,1024]{2,1,0:T(8,128)(2,1)} %lat_hbm.1, ...), custom_call_target="tpu_custom_call" | custom-call | flops 2000000000 | bytes 10000000 | tf_op jit(solution)/shard_map/banded_teacher/pallas_call | solution.py:452
  100.9 0.8 copy.10

commit v5 on v4

--- a/solution.py
+++ b/solution.py
@@ -12,7 +12,7 @@
 F32 = jnp.float32
 REACH = 4
 SPLIT = (96, 32)
-PIECE = (32, 16)
+PIECE = (48, 16)
 CH = len(SPLIT)
 START = (0, 96)
 PIECES = tuple(n // p for n, p in zip(SPLIT, PIECE))
@@ -407,7 +407,7 @@
     mix_remote(1, 2)
     pass_back(0, 1, (0,))
     pass_back(1, 2)
-    pass_back(0, 1, (1, 2))
+    pass_back(0, 1, (1,))
     mix_remote(1, 1)
     mix_own()
     pass_back(1, 1)

time: 103 us -> 103 us (level)
  no operation moved by 1% of the time
where the time goes in v5:
time: 103 us; the launch traced here: 102 us
  Pallas kernels  100 us (97%)
    pallas_call x1, Pallas kernels, shards(): pl.pallas_call(kernel, out_shape=pltpu.VMEM((1, tokens, student_width), F...  100 us

profile of v5, /device:TPU:8, one launch (start us, length us, event | category | flops | bytes accessed | tf_op | source)
XLA Modules:
  0.0 101.6 jit_solution(4934044236585827794)
XLA Ops:
  0.7 100.1 %banded_teacher.1 = f32[1,128,1024]{2,1,0:T(8,128)S(1)} custom-call(bf16[1,128,2560]{2,1,0:T(8,128)(2,1)} %q_hbm.1, bf16[1,128,2560]{2,1,0:T(8,128)(2,1)} %k_hbm.1, bf16[1,128,2560]{2,1,0:T(8,128)(2,1)} %v_hbm.1, s32[1,1]{1,0:T(1,128)S(6)} %copy.11.band_ref, f32[8,20]{1,0:T(8,128)} %bitcast.1, bf16[1,128,1024]{2,1,0:T(8,128)(2,1)} %lat_hbm.1, ...), custom_call_target="tpu_custom_call" | custom-call | flops 2000000000 | bytes 10000000 | tf_op jit(solution)/shard_map/banded_teacher/pallas_call | solution.py:452
  100.8 0.8 copy.10
